TPU v7x, 256 devices: a whole 4x4x8 slice. The times are simulated.
256 devices in a mesh: tok: 32 (over x_lo, z, core), voc: 8 (over y, x_hi).
Axes of the slice: x: 4 (x_hi: 2, x_lo: 2; x = x_hi * 2 + x_lo), y: 4, z: 8, core: 2. Of those that a mesh axis runs over, the one named last changes fastest.
Arguments:
- hidden: bfloat16 [4096, 1792], P('tok'), may hold values from -40 to 40
- head_weight: bfloat16 [1792, 131072], P(None, ('voc', 'tok')), may hold values from -0.37796447 to 0.37796447
- teacher_probs: bfloat16 [4096, 131072], P('tok', 'voc'), may hold values from 0 to 1, as said below
- teacher_row: int32 [4096], replicated, may hold values from 0 to 4095, each once
- lengths: int32 [32], replicated, may hold values from 1 to 128, as said below
Outputs:
- head_grad: bfloat16 [1792, 131072], P(None, ('voc', 'tok'))
Inputs may be any that keep to these rules, and one draw needn't show every extreme that they name: `teacher_row`: a permutation of the 4096 token positions. `lengths`: the last sequence is full. `teacher_probs`: each row is a probability distribution over the vocabulary: its entries sum to 1 up to rounding.
All inputs are finite; a program needn't handle non-finite values.
Results may differ from a plain program's by a relative error of at most 0.008.
Values may be sent and summed in bfloat16 or wider, within the bound.
No kernel may reach another device: no remote copies, remote signals or barrier semaphores. Data moves between devices by JAX's collectives and lax.ppermute only.
A program may use at most 128 MiB of HBM per device.

v0:
```python
import jax
import jax.numpy as jnp
from jax import lax
from jax.sharding import PartitionSpec as P

SEQ_LEN = 128


loss_scale = 1048576.0


def per_device(hidden, head_weight, teacher_probs, teacher_row, lengths):
    gathered = lax.all_gather(hidden, "tok", axis=0, tiled=True)
    logits = jnp.dot(gathered, head_weight, preferred_element_type=jnp.float32)
    teacher = lax.all_to_all(teacher_probs, "tok", split_axis=1, concat_axis=0, tiled=True)
    aligned = jnp.take(teacher, teacher_row, axis=0).astype(jnp.float32)
    local_peak = jnp.max(logits, axis=1)
    row_peak = lax.pmax(local_peak, ("tok", "voc"))
    row_total = lax.psum(jnp.sum(jnp.exp(logits - row_peak[:, None]), axis=1), ("tok", "voc"))
    log_student = logits - row_peak[:, None] - jnp.log(row_total)[:, None]
    student = jnp.exp(log_student)
    log_mix = jnp.log(0.5 * aligned + 0.5 * student)
    grad_prob = 0.5 * (log_student - log_mix)
    centre = lax.psum(jnp.sum(student * grad_prob, axis=1), ("tok", "voc"))
    rows_all = logits.shape[0]
    positions = jnp.arange(rows_all, dtype=jnp.int32)
    limits = jnp.repeat(lengths, SEQ_LEN, total_repeat_length=rows_all)
    valid_mask = (positions % SEQ_LEN < limits).astype(jnp.float32)
    token_count = jnp.sum(lengths).astype(jnp.float32)
    grad_scale = loss_scale / token_count
    dlogits = ((grad_scale * valid_mask)[:, None] * student * (grad_prob - centre[:, None])).astype(
        jnp.bfloat16
    )
    head_grad = lax.dot_general(
        gathered, dlogits, (((0,), (0,)), ((), ())), preferred_element_type=jnp.float32
    )
    return head_grad.astype(jnp.bfloat16)


def solution(mesh):
    return jax.shard_map(
        per_device,
        mesh=mesh,
        in_specs=(P("tok", None), P(None, ("voc", "tok")), P("tok", "voc"), P(), P()),
        out_specs=P(None, ("voc", "tok")),
        check_vma=False,
    )
```

profile of v0, /device:TPU:1, one launch (start us, length us, event | category | flops | bytes accessed | tf_op | source)
XLA Modules:
  0.0 470.6 jit_solution(12152239548933476016)
XLA Ops:
  6.5 0.0 copy-start
  6.5 0.0 all-gather.2.cloned.1.call-start
  6.5 0.7 all-gather.2.cloned.1.call-update
  7.3 0.0 copy-start.1
  7.3 0.0 copy-start.2
  7.3 4.8 %copy.11 = bf16[16,32,8,512]{3,2,0,1:T(8,128)(2,1)} copy(bf16[16,32,8,512]{3,2,1,0:T(8,128)(2,1)} %bitcast.60) | data formatting | bytes 8388608 | tf_op jit(solution)/shard_map/all_to_all | solution.py:15
  12.1 11.1 %all-to-all-start = ((bf16[128,32,512]{2,0,1:T(8,128)(2,1)}), bf16[128,32,512]{2,0,1:T(8,128)(2,1)}, u32[]{:S(2)}, u32[]{:S(2)}) async-start(bf16[128,32,512]{2,0,1:T(8,128)(2,1)} %bitcast.59), calls=%async_computation | async-start | bytes 8388608 | tf_op jit(solution)/shard_map/all_to_all | solution.py:15
  23.2 0.0 copy-done.1
  23.2 0.6 reduce_sum.27
  24.5 0.7 fusion.15
  25.2 0.7 fusion.14
  26.0 4.4 compare_select_fusion.1
  30.4 1.2 compare_reduce_fusion.24
  31.6 0.0 copy-done.2
  31.6 15.7 %fusion.10 = f32[4096]{0:T(1024)S(1)} fusion(pred[4096]{0:T(1024)(128)(4,1)S(1)} %get-tuple-element.41, pred[4096]{0:T(1024)(128)(4,1)S(1)} %get-tuple-element.40, pred[4096]{0:T(1024)(128)(4,1)S(1)} %get-tuple-element.39, pred[4096]{0:T(1024)(128)(4,1)S(1)} %get-tuple-element.38, pred[4096]{0:T(1024)(128)(4,1)S(1)} %get-tuple-element.37, ...), kind=kLoop, calls=%fused_computation.57 | loop fusion | flops 172032 | bytes 135272 | tf_op jit(solution)/shard_map/mul | solution.py:31
  47.3 109.5 %all-to-all-done = bf16[128,32,512]{2,0,1:T(8,128)(2,1)} async-done(((bf16[128,32,512]{2,0,1:T(8,128)(2,1)}), bf16[128,32,512]{2,0,1:T(8,128)(2,1)}, u32[]{:S(2)}, u32[]{:S(2)}) %all-to-all-start) | async-done | bytes 4194336 | tf_op jit(solution)/shard_map/all_to_all | solution.py:15
  156.9 20.2 %gather_fusion = bf16[4096,512]{1,0:T(8,128)(2,1)} fusion(bf16[4096,512]{1,0:T(8,128)(2,1)} %bitcast.38, s32[4096]{0:T(1024)S(1)} %fusion.11), kind=kCustom, calls=%fused_computation | custom fusion | bytes 8404992 | tf_op jit(solution)/shard_map/jit(_take)/gather | solution.py:16
  177.0 6.5 %copy.7 = bf16[4096,512]{0,1:T(8,128)(2,1)} copy(bf16[4096,512]{1,0:T(8,128)(2,1)} %gather_fusion) | data formatting | bytes 8388608 | tf_op jit(solution)/shard_map/jit(_take)/gather | solution.py:16
  183.6 7.8 %all-gather.2.cloned.1.call-done = bf16[4096,1792]{1,0:T(8,128)(2,1)} async-done(((bf16[128,1792]{1,0:T(8,128)(2,1)}), bf16[4096,1792]{1,0:T(8,128)(2,1)}) %all-gather.2.cloned.1.call-update) | async-done | bytes 14680080 | tf_op jit(solution)/shard_map/all_gather | solution.py:13
  191.4 0.0 copy-done
  191.4 13.1 %fusion.16 = (f32[4096]{0:T(1024)S(1)}, f32[4096,512]{0,1:T(8,128)}) fusion(bf16[4096,1792]{1,0:T(8,128)(2,1)} %all-gather.2.cloned.1.call-done, bf16[1792,512]{1,0:T(8,128)(2,1)S(1)} %copy-done), kind=kOutput, calls=%fused_computation.63 | convolution fusion | flops 7518285824 | bytes 24920064 | tf_op jit(solution)/shard_map/dot_general | solution.py:14
  204.5 78.3 %pmax.7 = f32[4096]{0:T(1024)S(1)} all-reduce(f32[4096]{0:T(1024)S(1)} %get-tuple-element.76), channel_id=1, replica_groups=mesh['tok'=32,'voc'=8] {'tok','voc'}, use_global_device_ids=true, to_apply=%region_2.3 | all-reduce | flops 4096 | bytes 32768 | tf_op jit(solution)/shard_map/pmax | solution.py:18
  282.8 4.5 exponential_reduce_fusion
  287.4 72.9 %psum.14 = f32[4096]{0:T(1024)S(1)} all-reduce(f32[4096]{0:T(1024)S(1)} %exponential_reduce_fusion), channel_id=1, replica_groups=mesh['tok'=32,'voc'=8] {'tok','voc'}, use_global_device_ids=true, to_apply=%region_4.5 | all-reduce | flops 4096 | bytes 32768 | tf_op jit(solution)/shard_map/psum | solution.py:19
  360.3 6.8 %multiply_reduce_fusion = f32[4096]{0:T(1024)S(1)} fusion(f32[4096,512]{0,1:T(8,128)} %get-tuple-element.77, f32[4096]{0:T(1024)S(1)} %log.6, f32[4096]{0:T(1024)S(1)} %pmax.7, bf16[4096,512]{0,1:T(8,128)(2,1)} %copy.7, pred[4096]{0:T(1024)(128)(4,1)S(1)} %compare_and_fusion), kind=kLoop, calls=%fused_computation.2 | loop fusion | flops 20967424 | bytes 12636160 | tf_op jit(solution)/shard_map/reduce_sum | solution.py:24
  367.1 73.8 %psum.15 = f32[4096]{0:T(1024)S(1)} all-reduce(f32[4096]{0:T(1024)S(1)} %multiply_reduce_fusion), channel_id=1, replica_groups=mesh['tok'=32,'voc'=8] {'tok','voc'}, use_global_device_ids=true, to_apply=%region_6.7 | all-reduce | flops 4096 | bytes 32768 | tf_op jit(solution)/shard_map/psum | solution.py:24
  440.9 19.1 %fusion.2 = bf16[1792,512]{0,1:T(8,128)(2,1)} fusion(bf16[4096,1792]{1,0:T(8,128)(2,1)} %all-gather.2.cloned.1.call-done, f32[4096,512]{0,1:T(8,128)} %get-tuple-element.77, f32[4096]{0:T(1024)S(1)} %psum.15, f32[4096]{0:T(1024)S(1)} %log.6, f32[4096]{0:T(1024)S(1)} %pmax.7, f32[4096]{0:T(1024)S(1)} %fusion.10, bf16[4096,512]{0,1:T(8,128)(2,1)} %copy.7, ...), kind=kOutput, calls=%fused_computation.10 | convolution fusion | flops 7542276096 | bytes 29167616 | tf_op jit(solution)/shard_map/dot_general | solution.py:34
  459.9 3.8 copy.8
  (5 shorter events, 0.0 us)
Async XLA Ops:
  6.5 184.8 %copy-start = (bf16[1792,512]{1,0:T(8,128)(2,1)S(1)}, bf16[1792,512]{1,0:T(8,128)(2,1)}, u32[]{:S(2)}) copy-start(bf16[1792,512]{1,0:T(8,128)(2,1)} %param.8) | copy-start | bytes 5505028
  6.5 184.8 %all-gather.2.cloned.1.call-start = ((), (), s32[]{:S(2)}) async-start(), calls=%async_computation.1 | async-start | bytes 15138816 | tf_op jit(solution)/shard_map/all_gather | solution.py:13
  7.3 15.9 %copy-start.1 = (s32[32]{0:T(128)S(1)}, s32[32]{0:T(128)}, u32[]{:S(2)}) copy-start(s32[32]{0:T(128)} %param.11) | copy-start | bytes 388
  7.3 24.3 %copy-start.2 = (s32[4096]{0:T(1024)S(1)}, s32[4096]{0:T(1024)}, u32[]{:S(2)}) copy-start(s32[4096]{0:T(1024)} %param.10) | copy-start | bytes 49156
  12.1 144.8 %all-to-all-start = ((bf16[128,32,512]{2,0,1:T(8,128)(2,1)}), bf16[128,32,512]{2,0,1:T(8,128)(2,1)}, u32[]{:S(2)}, u32[]{:S(2)}) async-start(bf16[128,32,512]{2,0,1:T(8,128)(2,1)} %bitcast.59), calls=%async_computation | async-start | bytes 8388608 | tf_op jit(solution)/shard_map/all_to_all | solution.py:15
Sparse Core Ops, SparseCore 0:
  9.2 182.1 all-gather.1
where the time goes:
time: 472 us; the launch traced here: 471 us
  blocking collectives  225 us (48%)
  waiting for transfers between devices  118 us (25%)
  local copies, waits for them, and re-layouts  36.8 us (8%)
  other arithmetic  33.3 us (7%)
  matrix products  32.2 us (7%)
  between operations  14.2 us (3%)
  starting transfers between devices  11.1 us (2%)
    all_to_all x1, waiting for transfers between devices, per_device(): lax.all_to_all(teacher_probs, 'tok', split_axis=1, concat_axis=0, tiled=T...  110 us
    pmax x1, blocking collectives, per_device(): row_peak = lax.pmax(local_peak, ('tok', 'voc'))  78.3 us
    psum x1, blocking collectives, per_device(): centre = lax.psum(jnp.sum(student * grad_prob, axis=1), ('tok', 'voc'))  73.8 us
    psum x1, blocking collectives, per_device(): lax.psum(jnp.sum(jnp.exp(logits - row_peak[:, None]), axis=1), ('tok', 'v...  72.9 us
    gather x2, local copies, waits for them, and re-layouts, per_device(): aligned = jnp.take(teacher, teacher_row, axis=0).astype(jnp.float32)  26.7 us
    dot_general x1, matrix products, per_device(): lax.dot_general(gathered, dlogits, (((0,), (0,)), ((), ())), preferred_el...  19.1 us
    mul x1, other arithmetic, per_device(): grad_scale * valid_mask  15.7 us
    dot_general x1, matrix products, per_device(): logits = jnp.dot(gathered, head_weight, preferred_element_type=jnp.float32)  13.1 us
  transfers between devices with their start and end apart: 2, of which 2 were waited for; matrix products, arithmetic and copies ran while one was open for 12% of the time, Pallas kernels for 0%

commit v1 on v0

v1 whole, which is shorter than its diff:
```python
import jax
import jax.numpy as jnp
from jax import lax
from jax.sharding import PartitionSpec as P

SEQ_LEN = 128


loss_scale = 1048576.0


def share_blocks(parts, tok, voc):
    k, rows = parts.shape
    blocks = parts.reshape(k, tok, rows // tok).transpose(1, 0, 2)
    return lax.all_to_all(blocks, "tok", split_axis=0, concat_axis=0, tiled=True)


def spread_blocks(block, tok, voc):
    k, part = block.shape
    copies = jnp.broadcast_to(block[None], (tok * voc, k, part))
    got = lax.all_to_all(copies, ("tok", "voc"), split_axis=0, concat_axis=0, tiled=True)
    return got.reshape(tok, voc, k, part).transpose(1, 2, 0, 3).reshape(voc, k, tok * part)


def merge_totals(peaks, totals):
    peak = jnp.max(peaks, axis=0)
    return peak, jnp.sum(totals * jnp.exp(peaks - peak[None]), axis=0)


def make_per_device(tok, voc):
    def per_device(hidden, head_weight, teacher_probs, teacher_row, lengths):
        gathered = lax.all_gather(hidden, "tok", axis=0, tiled=True)
        logits = jnp.dot(gathered, head_weight, preferred_element_type=jnp.float32)
        teacher = lax.all_to_all(teacher_probs, "tok", split_axis=1, concat_axis=0, tiled=True)
        aligned = jnp.take(teacher, teacher_row, axis=0).astype(jnp.float32)
        local_peak = jnp.max(logits, axis=1)
        local_total = jnp.sum(jnp.exp(logits - local_peak[:, None]), axis=1)
        terms = share_blocks(jnp.stack([local_peak, local_total]), tok, voc)
        terms = spread_blocks(jnp.stack(merge_totals(terms[:, 0], terms[:, 1])), tok, voc)
        row_peak, row_total = merge_totals(terms[:, 0], terms[:, 1])
        log_student = logits - row_peak[:, None] - jnp.log(row_total)[:, None]
        student = jnp.exp(log_student)
        log_mix = jnp.log(0.5 * aligned + 0.5 * student)
        grad_prob = 0.5 * (log_student - log_mix)
        local_centre = jnp.sum(student * grad_prob, axis=1)
        terms = share_blocks(local_centre[None], tok, voc)
        centre = jnp.sum(spread_blocks(jnp.sum(terms, axis=0), tok, voc), axis=0)[0]
        rows_all = logits.shape[0]
        positions = jnp.arange(rows_all, dtype=jnp.int32)
        limits = jnp.repeat(lengths, SEQ_LEN, total_repeat_length=rows_all)
        valid_mask = (positions % SEQ_LEN < limits).astype(jnp.float32)
        token_count = jnp.sum(lengths).astype(jnp.float32)
        grad_scale = loss_scale / token_count
        dlogits = ((grad_scale * valid_mask)[:, None] * student * (grad_prob - centre[:, None])).astype(
            jnp.bfloat16
        )
        head_grad = lax.dot_general(
            gathered, dlogits, (((0,), (0,)), ((), ())), preferred_element_type=jnp.float32
        )
        return head_grad.astype(jnp.bfloat16)

    return per_device


def solution(mesh):
    return jax.shard_map(
        make_per_device(mesh.shape["tok"], mesh.shape["voc"]),
        mesh=mesh,
        in_specs=(P("tok", None), P(None, ("voc", "tok")), P("tok", "voc"), P(), P()),
        out_specs=P(None, ("voc", "tok")),
        check_vma=False,
    )
```

time: 472 us -> 360 us (0.76)
  blocking collectives: 225 us -> 0 us
  waiting for transfers between devices: 118 us -> 200 us
  starting transfers between devices: 11.1 us -> 41.5 us
    psum x2 -> x0, blocking collectives: 147 us -> none  [the longest x1 73.8 us: per_device(): centre = lax.psum(jnp.sum(student * grad_prob, axis=1), ('tok', 'voc'))]
    all_gather x1, waiting for transfers between devices: 7.82 us -> 95.5 us  [per_device(): gathered = lax.all_gather(hidden, 'tok', axis=0, tiled=True)]
    pmax x1 -> x0, blocking collectives: 78.3 us -> none  [per_device(): row_peak = lax.pmax(local_peak, ('tok', 'voc'))]
    all_to_all x0 -> x4, starting transfers between devices: none -> 36.1 us  [the longest x2 19.5 us: spread_blocks(): lax.all_to_all(copies, ('tok', 'voc'), split_axis=0, concat_axis=0, tiled...]
    all_to_all x1, waiting for transfers between devices: 110 us -> 93.9 us  [per_device(): lax.all_to_all(teacher_probs, 'tok', split_axis=1, concat_axis=0, tiled=T...]
    all_to_all x0 -> x4, waiting for transfers between devices: none -> 9.63 us  [the longest x2 9.63 us: share_blocks(): lax.all_to_all(blocks, 'tok', split_axis=0, concat_axis=0, tiled=True)]
    all_to_all x1, starting transfers between devices: 11.1 us -> 5.35 us  [per_device(): lax.all_to_all(teacher_probs, 'tok', split_axis=1, concat_axis=0, tiled=T...]
    reduce_sum x2 -> x6, other arithmetic: 11.3 us -> 8.76 us  [the longest x1 7.36 us: per_device(): local_centre = jnp.sum(student * grad_prob, axis=1)]
  transfers between devices with their start and end apart: 2 -> 6, of which waited for: 2 -> 4; matrix products, arithmetic and copies ran while one was open for 12% -> 15% of each run, Pallas kernels for 0% -> 0%
where the time goes in v1:
time: 360 us; the launch traced here: 359 us
  waiting for transfers between devices  200 us (56%)
  local copies, waits for them, and re-layouts  41.5 us (12%)
  starting transfers between devices  41.5 us (12%)
  other arithmetic  31.6 us (9%)
  matrix products  30.2 us (8%)
  between operations  14.3 us (4%)
    all_gather x1, waiting for transfers between devices, per_device(): gathered = lax.all_gather(hidden, 'tok', axis=0, tiled=True)  95.5 us
    all_to_all x1, waiting for transfers between devices, per_device(): lax.all_to_all(teacher_probs, 'tok', split_axis=1, concat_axis=0, tiled=T...  93.9 us
    gather x2, local copies, waits for them, and re-layouts, per_device(): aligned = jnp.take(teacher, teacher_row, axis=0).astype(jnp.float32)  26.6 us
    all_to_all x2, starting transfers between devices, spread_blocks(): lax.all_to_all(copies, ('tok', 'voc'), split_axis=0, concat_axis=0, tiled...  19.5 us
    dot_general x1, matrix products, per_device(): lax.dot_general(gathered, dlogits, (((0,), (0,)), ((), ())), preferred_el...  19 us
    all_to_all x2, starting transfers between devices, share_blocks(): lax.all_to_all(blocks, 'tok', split_axis=0, concat_axis=0, tiled=True)  16.6 us
    mul x1, other arithmetic, per_device(): grad_scale * valid_mask  15.5 us
    dot_general x1, matrix products, per_device(): logits = jnp.dot(gathered, head_weight, preferred_element_type=jnp.float32)  11.2 us
  transfers between devices with their start and end apart: 6, of which 4 were waited for; matrix products, arithmetic and copies ran while one was open for 15% of the time, Pallas kernels for 0%

profile of v1, /device:TPU:1, one launch (start us, length us, event | category | flops | bytes accessed | tf_op | source)
XLA Modules:
  0.0 358.8 jit_solution(1625626498036616857)
XLA Ops:
  6.5 0.0 copy-start
  6.5 0.0 all-gather.2.cloned.1.call-start
  6.5 0.7 all-gather.2.cloned.1.call-update
  7.3 95.5 %all-gather.2.cloned.1.call-done = bf16[4096,1792]{1,0:T(8,128)(2,1)} async-done(((bf16[128,1792]{1,0:T(8,128)(2,1)}), bf16[4096,1792]{1,0:T(8,128)(2,1)}) %all-gather.2.cloned.1.call-update) | async-done | bytes 14680080 | tf_op jit(solution)/shard_map/all_gather | solution.py:32
  102.8 0.0 copy-done
  102.8 11.2 %fusion.21 = (f32[4096]{0:T(1024)S(1)}, f32[4096,512]{0,1:T(8,128)S(1)}) fusion(bf16[4096,1792]{1,0:T(8,128)(2,1)} %all-gather.2.cloned.1.call-done, bf16[1792,512]{1,0:T(8,128)(2,1)S(1)} %copy-done), kind=kOutput, calls=%fused_computation.76 | convolution fusion | flops 7518285824 | bytes 24920064 | tf_op jit(solution)/shard_map/dot_general | solution.py:33
  113.9 0.0 copy-start.1
  113.9 3.3 copy-done.1
  117.2 1.3 exponential_reduce_fusion
  118.5 0.7 maximum_bitcast_fusion
  119.1 7.3 %all-to-all-start = ((f32[32,2,128]{2,1,0:T(2,128)}), f32[32,2,128]{2,1,0:T(2,128)S(1)}, u32[]{:S(2)}, u32[]{:S(2)}) async-start(f32[32,2,128]{2,1,0:T(2,128)} %maximum_bitcast_fusion), calls=%async_computation | async-start | bytes 65536 | tf_op jit(solution)/shard_map/all_to_all | solution.py:15
  126.4 0.0 copy-start.2
  126.4 0.0 copy-start.3
  126.4 4.8 %copy.36 = bf16[16,32,8,512]{3,2,0,1:T(8,128)(2,1)} copy(bf16[16,32,8,512]{3,2,1,0:T(8,128)(2,1)} %bitcast.95) | data formatting | bytes 8388608 | tf_op jit(solution)/shard_map/all_to_all | solution.py:34
  131.2 3.1 all-to-all-done
  134.3 5.3 %all-to-all-start.2 = ((bf16[128,32,512]{2,0,1:T(8,128)(2,1)}), bf16[128,32,512]{2,0,1:T(8,128)(2,1)}, u32[]{:S(2)}, u32[]{:S(2)}) async-start(bf16[128,32,512]{2,0,1:T(8,128)(2,1)} %bitcast.94), calls=%async_computation.2 | async-start | bytes 8388608 | tf_op jit(solution)/shard_map/all_to_all | solution.py:34
  139.7 0.0 copy-done.2
  139.7 0.7 fusion.20
  140.5 93.9 %all-to-all-done.2 = bf16[128,32,512]{2,0,1:T(8,128)(2,1)} async-done(((bf16[128,32,512]{2,0,1:T(8,128)(2,1)}), bf16[128,32,512]{2,0,1:T(8,128)(2,1)}, u32[]{:S(2)}, u32[]{:S(2)}) %all-to-all-start.2) | async-done | bytes 4194336 | tf_op jit(solution)/shard_map/all_to_all | solution.py:34
  234.4 0.8 broadcast_in_dim.21
  235.2 11.6 %all-to-all-start.1 = ((f32[256,2,128]{2,1,0:T(2,128)}), f32[256,2,128]{2,1,0:T(2,128)S(1)}, u32[]{:S(2)}, u32[]{:S(2)}) async-start(f32[256,2,128]{2,1,0:T(2,128)} %broadcast_in_dim.21), calls=%async_computation.1 | async-start | bytes 524288 | tf_op jit(solution)/shard_map/all_to_all | solution.py:21
  246.8 4.7 %compare_select_fusion.1 = (s32[4096,1]{0,1:T(1,128)S(1)}, s32[4096,1]{0,1:T(1,128)S(1)}) fusion(s32[]{:T(128)} %bitcast.29, s32[]{:T(128)} %bitcast.30, s32[]{:T(128)} %bitcast.31, s32[]{:T(128)} %bitcast.32, s32[]{:T(128)} %bitcast.33, s32[]{:T(128)} %bitcast.35, s32[]{:T(128)} %bitcast.34, s32[4096,1]{0,1:T(1,128)S(1)} %bitcast.106, ...), kind=kLoop, calls=%fused_computation.47 | loop fusion | flops 57344 | bytes 65564 | tf_op jit(solution)/shard_map/jit(_take)/gather | solution.py:50
  251.5 0.0 copy-done.3
  251.5 20.1 %gather_fusion = bf16[4096,512]{1,0:T(8,128)(2,1)} fusion(bf16[4096,512]{1,0:T(8,128)(2,1)} %bitcast.52, s32[4096]{0:T(1024)S(1)} %fusion.15), kind=kCustom, calls=%fused_computation | custom fusion | bytes 8404992 | tf_op jit(solution)/shard_map/jit(_take)/gather | solution.py:35
  271.7 6.4 %copy.29 = bf16[4096,512]{0,1:T(8,128)(2,1)} copy(bf16[4096,512]{1,0:T(8,128)(2,1)} %gather_fusion) | data formatting | bytes 8388608 | tf_op jit(solution)/shard_map/jit(_take)/gather | solution.py:35
  278.1 0.0 all-to-all-done.1
  278.2 0.1 fusion.6
  278.2 7.4 %multiply_reduce_fusion = f32[4096]{0:T(1024)} fusion(f32[4096,512]{0,1:T(8,128)} %copy-done.1, f32[4096]{0:T(1024)S(1)} %log.10, f32[4096]{0:T(1024)S(1)} %slice_reduce_fusion, bf16[4096,512]{0,1:T(8,128)(2,1)} %copy.29, pred[4096]{0:T(1024)(128)(4,1)S(1)} %compare_and_fusion), kind=kLoop, calls=%fused_computation.2 | loop fusion | flops 20967424 | bytes 12636160 | tf_op jit(solution)/shard_map/reduce_sum | solution.py:45
  285.6 9.4 %all-to-all-start.3 = ((f32[32,1,128]{2,1,0:T(1,128)}), f32[32,1,128]{2,1,0:T(1,128)S(1)}, u32[]{:S(2)}, u32[]{:S(2)}) async-start(f32[32,1,128]{2,1,0:T(1,128)} %bitcast.53), calls=%async_computation.3 | async-start | bytes 32768 | tf_op jit(solution)/shard_map/all_to_all | solution.py:15
  295.0 1.2 compare_reduce_fusion.24
  296.2 6.6 %all-to-all-done.3 = f32[32,1,128]{2,1,0:T(1,128)S(1)} async-done(((f32[32,1,128]{2,1,0:T(1,128)}), f32[32,1,128]{2,1,0:T(1,128)S(1)}, u32[]{:S(2)}, u32[]{:S(2)}) %all-to-all-start.3) | async-done | bytes 16416 | tf_op jit(solution)/shard_map/all_to_all | solution.py:15
  302.8 0.7 broadcast_in_dim.27
  303.5 7.9 %all-to-all-start.4 = ((f32[256,1,128]{2,1,0:T(1,128)}), f32[256,1,128]{2,1,0:T(1,128)S(1)}, u32[]{:S(2)}, u32[]{:S(2)}) async-start(f32[256,1,128]{2,1,0:T(1,128)} %broadcast_in_dim.27), calls=%async_computation.4 | async-start | bytes 262144 | tf_op jit(solution)/shard_map/all_to_all | solution.py:21
  311.5 0.7 fusion.19
  312.2 0.7 reduce_sum.63
  313.5 15.5 %fusion.14 = f32[4096]{0:T(1024)S(1)} fusion(pred[4096]{0:T(1024)(128)(4,1)S(1)} %get-tuple-element.41, pred[4096]{0:T(1024)(128)(4,1)S(1)} %get-tuple-element.40, pred[4096]{0:T(1024)(128)(4,1)S(1)} %get-tuple-element.39, pred[4096]{0:T(1024)(128)(4,1)S(1)} %get-tuple-element.38, pred[4096]{0:T(1024)(128)(4,1)S(1)} %get-tuple-element.37, ...), kind=kLoop, calls=%fused_computation.68 | loop fusion | flops 172032 | bytes 135272 | tf_op jit(solution)/shard_map/mul | solution.py:54
  329.1 0.0 all-to-all-done.4
  329.1 19.0 %fusion.3 = bf16[1792,512]{0,1:T(8,128)(2,1)} fusion(bf16[4096,1792]{1,0:T(8,128)(2,1)} %all-gather.2.cloned.1.call-done, f32[4096,512]{0,1:T(8,128)} %copy-done.1, f32[4096]{0:T(1024)S(1)} %bitcast.108, f32[4096]{0:T(1024)S(1)} %log.10, f32[4096]{0:T(1024)S(1)} %slice_reduce_fusion, f32[4096]{0:T(1024)S(1)} %fusion.14, bf16[4096,512]{0,1:T(8,128)(2,1)} %copy.29, ...), kind=kOutput, calls=%fused_computation.11 | convolution fusion | flops 7542276096 | bytes 29167616 | tf_op jit(solution)/shard_map/dot_general | solution.py:57
  348.1 3.8 %copy.31 = bf16[1792,512]{1,0:T(8,128)(2,1)} copy(bf16[1792,512]{0,1:T(8,128)(2,1)} %fusion.3) | data formatting | bytes 3670016 | tf_op jit(solution)/shard_map/convert_element_type | solution.py:60
  (13 shorter events, 0.2 us)
Async XLA Ops:
  6.5 96.2 %copy-start = (bf16[1792,512]{1,0:T(8,128)(2,1)S(1)}, bf16[1792,512]{1,0:T(8,128)(2,1)}, u32[]{:S(2)}) copy-start(bf16[1792,512]{1,0:T(8,128)(2,1)} %param.8) | copy-start | bytes 5505028
  6.5 96.2 %all-gather.2.cloned.1.call-start = ((), (), s32[]{:S(2)}) async-start(), calls=%async_computation.5 | async-start | bytes 15138816 | tf_op jit(solution)/shard_map/all_gather | solution.py:32
  113.9 3.3 copy-start.1
  119.1 15.2 %all-to-all-start = ((f32[32,2,128]{2,1,0:T(2,128)}), f32[32,2,128]{2,1,0:T(2,128)S(1)}, u32[]{:S(2)}, u32[]{:S(2)}) async-start(f32[32,2,128]{2,1,0:T(2,128)} %maximum_bitcast_fusion), calls=%async_computation | async-start | bytes 65536 | tf_op jit(solution)/shard_map/all_to_all | solution.py:15
  126.4 13.3 %copy-start.2 = (s32[32]{0:T(128)S(1)}, s32[32]{0:T(128)}, u32[]{:S(2)}) copy-start(s32[32]{0:T(128)} %param.11) | copy-start | bytes 388
  126.4 125.1 %copy-start.3 = (s32[4096]{0:T(1024)S(1)}, s32[4096]{0:T(1024)}, u32[]{:S(2)}) copy-start(s32[4096]{0:T(1024)} %param.10) | copy-start | bytes 49156
  134.3 100.1 %all-to-all-start.2 = ((bf16[128,32,512]{2,0,1:T(8,128)(2,1)}), bf16[128,32,512]{2,0,1:T(8,128)(2,1)}, u32[]{:S(2)}, u32[]{:S(2)}) async-start(bf16[128,32,512]{2,0,1:T(8,128)(2,1)} %bitcast.94), calls=%async_computation.2 | async-start | bytes 8388608 | tf_op jit(solution)/shard_map/all_to_all | solution.py:34
  235.2 42.9 %all-to-all-start.1 = ((f32[256,2,128]{2,1,0:T(2,128)}), f32[256,2,128]{2,1,0:T(2,128)S(1)}, u32[]{:S(2)}, u32[]{:S(2)}) async-start(f32[256,2,128]{2,1,0:T(2,128)} %broadcast_in_dim.21), calls=%async_computation.1 | async-start | bytes 524288 | tf_op jit(solution)/shard_map/all_to_all | solution.py:21
  285.6 17.2 %all-to-all-start.3 = ((f32[32,1,128]{2,1,0:T(1,128)}), f32[32,1,128]{2,1,0:T(1,128)S(1)}, u32[]{:S(2)}, u32[]{:S(2)}) async-start(f32[32,1,128]{2,1,0:T(1,128)} %bitcast.53), calls=%async_computation.3 | async-start | bytes 32768 | tf_op jit(solution)/shard_map/all_to_all | solution.py:15
  303.5 25.6 %all-to-all-start.4 = ((f32[256,1,128]{2,1,0:T(1,128)}), f32[256,1,128]{2,1,0:T(1,128)S(1)}, u32[]{:S(2)}, u32[]{:S(2)}) async-start(f32[256,1,128]{2,1,0:T(1,128)} %broadcast_in_dim.27), calls=%async_computation.4 | async-start | bytes 262144 | tf_op jit(solution)/shard_map/all_to_all | solution.py:21
Sparse Core Ops, SparseCore 0:
  9.2 93.5 all-gather.1
